TPU v7x, 32 devices: a whole 2x2x4 slice. The times are simulated.
32 devices in a mesh: groups: 2 (over x), out: 8 (over z, y), inp: 2 (over core).
Axes of the slice: x: 2, y: 2, z: 4, core: 2. Of those that a mesh axis runs over, the one named last changes fastest.
Arguments:
- pool: bfloat16 [8192, 5120], P('groups', 'out'), parts along dimension 0, may hold values from -6 to 6
- token_ids: int32 [384, 16], P(('groups', 'inp')), parts along dimension 0, may hold values from 0 to 4095
- weight: bfloat16 [5120, 27648], P('inp', 'out'), may hold values from -0.078125 to 0.078125
- factor_a: bfloat16 [384, 5120], P(('groups', 'inp'), 'out'), parts along dimension 0, may hold values from -6 to 6
- factor_b: bfloat16 [384, 27648], P(('groups', 'inp'), 'out'), parts along dimension 0, may hold values from -6 to 6
- ranks: int32 [384], P('groups'), parts along dimension 0, may hold values from 0 to 191, each once
Outputs:
- outputs: bfloat16 [6144, 27648], P(('groups', 'inp'), 'out'), parts along dimension 0
- direction: bfloat16 [10240, 27648], P(('groups', 'inp'), 'out'), parts along dimension 0
There are 2 independent parts, one for each index of `groups`. A program takes and returns all parts, laid end to end along the dimension named above; an argument that names none is the same for every part. Nothing has to cross between parts.
Inputs may be any that keep to these rules, and one draw needn't show every extreme that they name: `ranks`: each of 0 to 191 once.
All inputs are finite; a program needn't handle non-finite values.
Results may differ from a plain program's by a relative error of at most 0.005.
Values may be sent and summed in bfloat16 or wider, within the bound.
A program may use at most 384 MiB of HBM per device.

v0:
```python
import functools
import math

import jax
import jax.numpy as jnp
from jax import lax
from jax.experimental import pallas as pl
from jax.experimental.pallas import tpu as pltpu
from jax.sharding import PartitionSpec as P

D = 5120
SEQ = 16
TILE = 256
F32 = jnp.float32
BF16 = jnp.bfloat16


def ring_order(n):
    if n <= 8:
        return list(range(0, n, 2)) + list(range(1, n, 2))[::-1]
    return list(range(n))


def block_kernel(n_blocks, has_acc, last, half_tiles, own_ref, *refs):
    refs = list(refs)
    tops = [refs.pop(0) for _ in range(n_blocks)]
    bottoms = [refs.pop(0) for _ in range(n_blocks)]
    factors = [refs.pop(0) for _ in range(n_blocks)]
    weight_ref = refs.pop(0)
    acc_ref, reach_in = (refs.pop(0), refs.pop(0)) if has_acc else (None, None)
    b_ref = refs.pop(0) if last else None
    out_ref = refs.pop(0)
    reach_out = None if last else refs.pop(0)
    held, sems = refs
    step = pl.program_id(0)
    width = tops[0].shape[1]
    members = factors[0].shape[0]

    @pl.when(step == 0)
    def _():
        copies = [
            pltpu.make_async_copy(
                weight_ref.at[pl.ds(pl.multiple_of(own_ref[k] * width, width), width)],
                held.at[pl.ds(k * width, width)],
                sems.at[k],
            )
            for k in range(n_blocks)
        ]
        for copy in copies:
            copy.start()
        if last:
            for k in range(2):
                held[pl.ds(n_blocks * width + k * members, members), :] = b_ref[...]
        for copy in copies:
            copy.wait()

    def run(rows):
        blocks = [r_ref[...] for r_ref in rows]
        reach = reach_in[...] if has_acc else None
        for r, a_ref in zip(blocks, factors):
            part = lax.dot_general(
                r, a_ref[...], (((1,), (1,)), ((), ())), preferred_element_type=F32
            )
            reach = part if reach is None else reach + part
        if last:
            member = (lax.broadcasted_iota(jnp.int32, reach.shape, 0) + step * TILE) // SEQ
            own = lax.broadcasted_iota(jnp.int32, reach.shape, 1) == member
            scaled = jnp.where(own, reach * (0.5 / math.sqrt(D)), 0.0)
            high = scaled.astype(BF16)
            low = (scaled - high.astype(F32)).astype(BF16)
            blocks += [high, low]
        left = blocks[0] if len(blocks) == 1 else jnp.concatenate(blocks, axis=1)
        total = jnp.dot(left, held[...], preferred_element_type=F32)
        if has_acc:
            total = total + acc_ref[...]
        out_ref[...] = total.astype(out_ref.dtype)
        if not last:
            reach_out[...] = reach

    @pl.when(step < half_tiles)
    def _():
        run(tops)

    @pl.when(step >= half_tiles)
    def _():
        run(bottoms)


def add_blocks(owners, tops, bottoms, factors, weight, acc=None, factor_b=None):
    n_blocks = len(tops)
    half, width = tops[0].shape
    cols = weight.shape[1]
    members = factors[0].shape[0]
    half_tiles = half // TILE
    last = factor_b is not None
    rows = 2 * half

    def whole(shape):
        return pl.BlockSpec(shape, lambda i, own: (0, 0))

    def tile(width):
        return pl.BlockSpec((TILE, width), lambda i, own: (i, 0))

    specs = [
        pl.BlockSpec((TILE, width), lambda i, own: (jnp.minimum(i, half_tiles - 1), 0))
        for _ in tops
    ]
    specs += [
        pl.BlockSpec((TILE, width), lambda i, own: (jnp.maximum(i - half_tiles, 0), 0))
        for _ in bottoms
    ]
    specs += [whole((members, width)) for _ in factors]
    specs.append(pl.BlockSpec(memory_space=pl.ANY))
    operands = list(tops) + list(bottoms) + list(factors) + [weight]
    if acc is not None:
        specs += [tile(cols), tile(members)]
        operands += list(acc)
    if last:
        specs.append(whole((members, cols)))
        operands.append(factor_b)
        out_shape = jax.ShapeDtypeStruct((rows, cols), BF16)
        out_specs = tile(cols)
    else:
        out_shape = (
            jax.ShapeDtypeStruct((rows, cols), F32),
            jax.ShapeDtypeStruct((rows, members), F32),
        )
        out_specs = (tile(cols), tile(members))
    depth = n_blocks * width + (2 * members if last else 0)
    traffic = n_blocks * width * (rows + cols) * 2 + rows * cols * (
        (4 if acc is not None else 0) + (2 if last else 4)
    )
    return pl.pallas_call(
        functools.partial(block_kernel, n_blocks, acc is not None, last, half_tiles),
        grid_spec=pltpu.PrefetchScalarGridSpec(
            num_scalar_prefetch=1,
            grid=(rows // TILE,),
            in_specs=specs,
            out_specs=out_specs,
            scratch_shapes=[
                pltpu.VMEM((depth, cols), BF16),
                pltpu.SemaphoreType.DMA((n_blocks,)),
            ],
        ),
        out_shape=out_shape,
        cost_estimate=pl.CostEstimate(
            flops=2 * rows * depth * cols, bytes_accessed=traffic, transcendentals=0
        ),
        compiler_params=pltpu.CompilerParams(vmem_limit_bytes=56 * 1024 * 1024),
    )(owners, *operands)


def per_device(n, n_inp, pool, token_ids, weight, factor_a, factor_b, ranks):
    mem_local = factor_a.shape[0]
    members = ranks.shape[0]
    rows = mem_local * SEQ
    half = rows // 2
    width = pool.shape[1]
    inp_index = lax.axis_index("inp")
    me = lax.axis_index("out")

    order = ring_order(n)
    place = [order.index(j) for j in range(n)]
    up = [(order[k], order[(k + 1) % n]) for k in range(n)]
    down = [(order[(k + 1) % n], order[k]) for k in range(n)]
    owners = [[order[(place[j] + s) % n] for s in range(-(n // 2), n // 2)] for j in range(n)]
    slots = [[row.index(j) for j in range(n)] for row in owners]
    table = lax.dynamic_index_in_dim(
        jnp.array([r + q for r, q in zip(owners, slots)], jnp.int32), me, 0, keepdims=False
    )

    def send(x, perm):
        return lax.ppermute(x, "out", perm)

    swap = [(0, 1), (1, 0)]

    lanes = -(-mem_local // 128) * 128
    pad = ((0, lanes - mem_local), (0, 0))
    a_of = {0: factor_a}
    for s in range(1, n // 2 + 1):
        a_of[-s] = send(a_of[-(s - 1)], up)
        if s < n // 2:
            a_of[s] = send(a_of[s - 1], down)
    b_other = lax.ppermute(factor_b, "inp", swap)

    ids = token_ids.reshape(-1)
    top, bottom = pool[ids[:half]], pool[ids[half:]]
    w_all = lax.all_gather(weight, "inp", axis=0, tiled=True)

    stacked = jnp.stack([a_of[s] for s in range(-(n // 2), n // 2)])
    per_half = n // n_inp

    def features(which):
        pieces = []
        mine = lax.dynamic_slice_in_dim(table, n + which * per_half, per_half)
        for k in range(per_half):
            pieces.append(lax.dynamic_index_in_dim(stacked, mine[k], 0, keepdims=False))
        return jnp.concatenate(pieces, axis=1)

    a_own = features(inp_index)
    a_other = lax.ppermute(features(1 - inp_index), "inp", swap)
    shaping = 2.0 * ranks.astype(F32) / (members - 1) - 1.0
    norm_factor = 1.0 / math.sqrt(members)

    def scale(which, b):
        part = lax.dynamic_slice_in_dim(shaping, which * mem_local, mem_local, 0)
        return (part[:, None] * b.astype(F32) * norm_factor).astype(BF16)

    scaled = jnp.concatenate([scale(inp_index, factor_b), scale(1 - inp_index, b_other)], axis=0)
    a_pair = jnp.concatenate([a_own, a_other], axis=0)
    direction = lax.dot_general(
        a_pair, scaled, (((0,), (0,)), ((), ())), preferred_element_type=F32
    ).astype(BF16)

    def blocks(shifts, acc=None, b=None):
        return add_blocks(
            jnp.concatenate([table[s + n // 2 : s + n // 2 + 1] for s in shifts]),
            [tops[s] for s in shifts],
            [bottoms[s] for s in shifts],
            [jnp.pad(a_of[s], pad) for s in shifts],
            w_all,
            acc,
            b,
        )

    tops, bottoms = {0: top}, {0: bottom}
    acc = None
    for s in range(1, n // 2 + 1):
        if s >= 3:
            acc = blocks([0, -1, 1]) if s == 3 else blocks([2 - s, s - 2], acc)
            ready = (tops[1 - s], tops[s - 1], bottoms[1 - s], bottoms[s - 1])
            ready, acc = lax.optimization_barrier((ready, acc))
            tops[1 - s], tops[s - 1], bottoms[1 - s], bottoms[s - 1] = ready
        tops[-s] = send(tops[-(s - 1)], up)
        bottoms[s] = send(bottoms[s - 1], down)
        if s < n // 2:
            tops[s] = send(tops[s - 1], down)
            bottoms[-s] = send(bottoms[-(s - 1)], up)
    bottoms[-(n // 2)] = bottoms[n // 2]
    acc = blocks([1 - n // 2, n // 2 - 1], acc)
    outputs = blocks([-(n // 2)], acc, jnp.pad(factor_b, pad))
    return (outputs, direction)


def solution(mesh):
    placed = (
        P("groups", "out"),
        P(("groups", "inp"), None),
        P("inp", "out"),
        P(("groups", "inp"), "out"),
        P(("groups", "inp"), "out"),
        P("groups"),
    )
    return jax.shard_map(
        functools.partial(per_device, mesh.shape["out"], mesh.shape["inp"]),
        mesh=mesh,
        in_specs=placed,
        out_specs=(P(("groups", "inp"), "out"), P(("groups", "inp"), "out")),
        check_vma=False,
    )
```

profile of v0, /device:TPU:0, one launch (start us, length us, event | category | flops | bytes accessed | tf_op | source)
XLA Modules:
  0.0 274.1 jit_solution(18137393676922543305)
XLA Ops:
  8.4 6.1 %gather_fusion = bf16[768,640]{1,0:T(8,128)(2,1)S(1)} fusion(bf16[4096,640]{1,0:T(8,128)(2,1)} %param.7, s32[1024]{0:T(1024)S(1)} %pad_clamp_fusion.1), kind=kCustom, calls=%fused_computation | custom fusion | bytes 1969152 | tf_op jit(solution)/shard_map/gather | solution.py:187
  14.5 3.1 %collective-permute-start = (bf16[768,640]{1,0:T(8,128)(2,1)S(1)}, bf16[768,640]{1,0:T(8,128)(2,1)}, u32[]{:S(2)}, u32[]{:S(2)}) collective-permute-start(bf16[768,640]{1,0:T(8,128)(2,1)S(1)} %gather_fusion), channel_id=1, source_target_pairs={{0,4},{4,8},{8,12},{12,14},{14,10},{10,6},{6,2},{2,0},{1,5},{5,9},... | collective-permute-start | bytes 2949128 | tf_op jit(solution)/shard_map/ppermute | solution.py:173
  17.6 2.0 collective-permute-start.8
  19.7 8.0 %gather_fusion.1 = bf16[768,640]{1,0:T(8,128)(2,1)S(1)} fusion(bf16[4096,640]{1,0:T(8,128)(2,1)} %param.7, s32[1024]{0:T(1024)S(1)} %pad_clamp_fusion), kind=kCustom, calls=%fused_computation.1 | custom fusion | bytes 1969152 | tf_op jit(solution)/shard_map/gather | solution.py:187
  27.7 2.1 collective-permute-start.4
  31.0 11.8 %collective-permute-done.8 = bf16[96,640]{1,0:T(8,128)(2,1)} collective-permute-done((bf16[96,640]{1,0:T(8,128)(2,1)S(1)}, bf16[96,640]{1,0:T(8,128)(2,1)}, u32[]{:S(2)}, u32[]{:S(2)}) %collective-permute-start.8) | collective-permute-done | bytes 122912 | tf_op jit(solution)/shard_map/ppermute | solution.py:173
  42.9 2.1 collective-permute-start.14
  46.4 19.2 %collective-permute-done.14 = bf16[96,640]{1,0:T(8,128)(2,1)S(1)} collective-permute-done((bf16[96,640]{1,0:T(8,128)(2,1)}, bf16[96,640]{1,0:T(8,128)(2,1)S(1)}, u32[]{:S(2)}, u32[]{:S(2)}) %collective-permute-start.14) | collective-permute-done | bytes 122912 | tf_op jit(solution)/shard_map/ppermute | solution.py:173
  65.6 1.8 collective-permute-start.18
  67.4 1.7 pad_add_fusion.1.own_ref
  70.6 1.8 collective-permute-start.19
  72.4 1.7 pad_add_fusion.2.own_ref
  91.0 2.6 pad_add_fusion.own_ref
  110.3 1.8 collective-permute-start.1
  112.4 1.8 collective-permute-start.5
  114.2 11.2 %collective-permute-done.6.refs_5_ = bf16[768,640]{1,0:T(8,128)(2,1)} collective-permute-done((bf16[768,640]{1,0:T(8,128)(2,1)S(1)}, bf16[768,640]{1,0:T(8,128)(2,1)}, u32[]{:S(2)}, u32[]{:S(2)}) %collective-permute-start.6) | collective-permute-done | bytes 983072 | tf_op jit(solution)/shard_map/ppermute | solution.py:173
  126.4 10.1 %convolution_convert_fusion = bf16[2560,3456]{1,0:T(8,128)(2,1)} fusion(bf16[96,3456]{1,0:T(8,128)(2,1)S(1)} %multiply_convert_fusion, bf16[96,3456]{1,0:T(8,128)(2,1)S(1)} %multiply_convert_fusion.1, bf16[96,2560]{1,0:T(8,128)(2,1)} %copy-done.11, bf16[96,640]{1,0:T(8,128)(2,1)S(1)} %get-tuple-element.43, bf16[96,640]{1,0:T(8,128)(2,1)} %get-tuple-element.44, ...), kind=kOutput, calls=%fused_computation.2 | convolution fusion | flops 3413803008 | bytes 20004864 | tf_op jit(solution)/shard_map/dot_general | solution.py:211
  136.5 34.8 %shard_map.86 = (f32[1536,3456]{1,0:T(8,128)}, f32[1536,128]{1,0:T(8,128)}) custom-call(s32[3]{0:T(128)} %pad_add_fusion.own_ref, bf16[768,640]{1,0:T(8,128)(2,1)} %copy-done.1, bf16[768,640]{1,0:T(8,128)(2,1)} %collective-permute-done.refs_1_, bf16[768,640]{1,0:T(8,128)(2,1)} %collective-permute-done.2.refs_2_, bf16[768,640]{1,0:T(8,128)(2,1)} %copy-done.2, ...), custom_call_target="tpu_custom_call" | custom-call | flops 20384317440 | bytes 40402944 | tf_op jit(solution)/shard_map/pallas_call | solution.py:133
  171.5 1.8 collective-permute-start.10
  173.5 1.8 collective-permute-start.12
  175.6 27.2 %shard_map.87 = (f32[1536,3456]{1,0:T(8,128)}, f32[1536,128]{1,0:T(8,128)}) custom-call(s32[2]{0:T(128)} %pad_add_fusion.1.own_ref, bf16[768,640]{1,0:T(8,128)(2,1)} %collective-permute-done.1.refs_0_, bf16[768,640]{1,0:T(8,128)(2,1)} %copy-done.3, bf16[768,640]{1,0:T(8,128)(2,1)} %collective-permute-done.5.refs_2_, bf16[768,640]{1,0:T(8,128)(2,1)} %copy-done.4, ...), custom_call_target="tpu_custom_call" | custom-call | flops 13589544960 | bytes 55246848 | tf_op jit(solution)/shard_map/pallas_call | solution.py:133
  202.8 11.8 %collective-permute-done.12.refs_2_ = bf16[768,640]{1,0:T(8,128)(2,1)S(1)} collective-permute-done((bf16[768,640]{1,0:T(8,128)(2,1)}, bf16[768,640]{1,0:T(8,128)(2,1)S(1)}, u32[]{:S(2)}, u32[]{:S(2)}) %collective-permute-start.12) | collective-permute-done | bytes 983072 | tf_op jit(solution)/shard_map/ppermute | solution.py:173
  217.0 27.3 %shard_map.88 = (f32[1536,3456]{1,0:T(8,128)}, f32[1536,128]{1,0:T(8,128)}) custom-call(s32[2]{0:T(128)} %pad_add_fusion.2.own_ref, bf16[768,640]{1,0:T(8,128)(2,1)} %copy-done.5, bf16[768,640]{1,0:T(8,128)(2,1)} %copy-done.6, bf16[768,640]{1,0:T(8,128)(2,1)} %copy-done.8, bf16[768,640]{1,0:T(8,128)(2,1)} %copy-done.7, bf16[128,640]{1,0:T(8,128)(2,1)} %pad.35.refs_4_, ...), custom_call_target="tpu_custom_call" | custom-call | flops 13589544960 | bytes 55246848 | tf_op jit(solution)/shard_map/pallas_call | solution.py:133
  245.6 21.6 %shard_map.89 = bf16[1536,3456]{1,0:T(8,128)(2,1)} custom-call(s32[1]{0:T(128)} %bitcast.own_ref, bf16[768,640]{1,0:T(8,128)(2,1)} %copy-done.9, bf16[768,640]{1,0:T(8,128)(2,1)} %copy-done.10, bf16[128,640]{1,0:T(8,128)(2,1)} %pad.34.refs_2_, bf16[5120,3456]{1,0:T(8,128)(2,1)} %all-gather.2.cloned.1.call-done.refs_9_.refs_6_.refs_3_, ...), custom_call_target="tpu_custom_call" | custom-call | flops 9512681472 | bytes 38240256 | tf_op jit(solution)/shard_map/pallas_call | solution.py:133
  (104 shorter events, 29.0 us)
Async XLA Ops:
  7.2 129.4 %all-gather.2.cloned.1.call-start = ((), (), s32[]{:S(2)}) async-start(), calls=%async_computation | async-start | bytes 53084160 | tf_op jit(solution)/shard_map/all_gather | solution.py:188
  14.5 95.7 %collective-permute-start = (bf16[768,640]{1,0:T(8,128)(2,1)S(1)}, bf16[768,640]{1,0:T(8,128)(2,1)}, u32[]{:S(2)}, u32[]{:S(2)}) collective-permute-start(bf16[768,640]{1,0:T(8,128)(2,1)S(1)} %gather_fusion), channel_id=1, source_target_pairs={{0,4},{4,8},{8,12},{12,14},{14,10},{10,6},{6,2},{2,0},{1,5},{5,9},... | collective-permute-start | bytes 2949128 | tf_op jit(solution)/shard_map/ppermute | solution.py:173
  17.6 94.5 %collective-permute-start.2 = (bf16[768,640]{1,0:T(8,128)(2,1)S(1)}, bf16[768,640]{1,0:T(8,128)(2,1)}, u32[]{:S(2)}, u32[]{:S(2)}) collective-permute-start(bf16[768,640]{1,0:T(8,128)(2,1)S(1)} %gather_fusion), channel_id=1, source_target_pairs={{4,0},{8,4},{12,8},{14,12},{10,14},{6,10},{2,6},{0,2},{5,1},{9,5},... | collective-permute-start | bytes 2949128 | tf_op jit(solution)/shard_map/ppermute | solution.py:173
  17.6 25.3 %collective-permute-start.8 = (bf16[96,640]{1,0:T(8,128)(2,1)S(1)}, bf16[96,640]{1,0:T(8,128)(2,1)}, u32[]{:S(2)}, u32[]{:S(2)}) collective-permute-start(bf16[96,640]{1,0:T(8,128)(2,1)S(1)} %copy-done.12), channel_id=1, source_target_pairs={{0,4},{4,8},{8,12},{12,14},{14,10},{10,6},{6,2},{2,0},{1,5},{5,9},... | collective-permute-start | bytes 368648 | tf_op jit(solution)/shard_map/ppermute | solution.py:173
  19.6 26.7 %collective-permute-start.9 = (bf16[96,640]{1,0:T(8,128)(2,1)S(1)}, bf16[96,640]{1,0:T(8,128)(2,1)S(1)}, u32[]{:S(2)}, u32[]{:S(2)}) collective-permute-start(bf16[96,640]{1,0:T(8,128)(2,1)S(1)} %copy-done.12), channel_id=1, source_target_pairs={{4,0},{8,4},{12,8},{14,12},{10,14},{6,10},{2,6},{0,2},{5,1},{9,5},... | collective-permute-start | bytes 368648 | tf_op jit(solution)/shard_map/ppermute | solution.py:173
  27.7 84.6 %collective-permute-start.4 = (bf16[768,640]{1,0:T(8,128)(2,1)S(1)}, bf16[768,640]{1,0:T(8,128)(2,1)}, u32[]{:S(2)}, u32[]{:S(2)}) collective-permute-start(bf16[768,640]{1,0:T(8,128)(2,1)S(1)} %gather_fusion.1), channel_id=1, source_target_pairs={{0,4},{4,8},{8,12},{12,14},{14,10},{10,6},{6,2},{2,0},{1,5},{5,9},... | collective-permute-start | bytes 2949128 | tf_op jit(solution)/shard_map/ppermute | solution.py:173
  42.9 22.8 %collective-permute-start.14 = (bf16[96,640]{1,0:T(8,128)(2,1)}, bf16[96,640]{1,0:T(8,128)(2,1)S(1)}, u32[]{:S(2)}, u32[]{:S(2)}) collective-permute-start(bf16[96,640]{1,0:T(8,128)(2,1)} %collective-permute-done.8), channel_id=1, source_target_pairs={{0,4},{4,8},{8,12},{12,14},{14,10},{10,6},{6,2},{2,0},{1,5},{5,9},... | collective-permute-start | bytes 368648 | tf_op jit(solution)/shard_map/ppermute | solution.py:173
  46.4 23.4 %collective-permute-start.15 = (bf16[96,640]{1,0:T(8,128)(2,1)S(1)}, bf16[96,640]{1,0:T(8,128)(2,1)}, u32[]{:S(2)}, u32[]{:S(2)}) collective-permute-start(bf16[96,640]{1,0:T(8,128)(2,1)S(1)} %collective-permute-done.9), channel_id=1, source_target_pairs={{4,0},{8,4},{12,8},{14,12},{10,14},{6,10},{2,6},{0,2},{5,1},{9,5},... | collective-permute-start | bytes 368648 | tf_op jit(solution)/shard_map/ppermute | solution.py:173
  65.6 5.0 %collective-permute-start.18 = (bf16[96,640]{1,0:T(8,128)(2,1)S(1)}, bf16[96,640]{1,0:T(8,128)(2,1)}, u32[]{:S(2)}, u32[]{:S(2)}) collective-permute-start(bf16[96,640]{1,0:T(8,128)(2,1)S(1)} %collective-permute-done.14), channel_id=1, source_target_pairs={{0,4},{4,8},{8,12},{12,14},{14,10},{10,6},{6,2},{2,0},{1,5},{5,9},... | collective-permute-start | bytes 368648 | tf_op jit(solution)/shard_map/ppermute | solution.py:173
  69.8 30.7 %collective-permute-start.20 = (bf16[96,640]{1,0:T(8,128)(2,1)}, bf16[96,640]{1,0:T(8,128)(2,1)}, u32[]{:S(2)}, u32[]{:S(2)}) collective-permute-start(bf16[96,640]{1,0:T(8,128)(2,1)} %collective-permute-done.15), channel_id=1, source_target_pairs={{4,0},{8,4},{12,8},{14,12},{10,14},{6,10},{2,6},{0,2},{5,1},{9,5},... | collective-permute-start | bytes 368648 | tf_op jit(solution)/shard_map/ppermute | solution.py:173
  70.6 31.8 %collective-permute-start.19 = (bf16[96,640]{1,0:T(8,128)(2,1)}, bf16[96,640]{1,0:T(8,128)(2,1)}, u32[]{:S(2)}, u32[]{:S(2)}) collective-permute-start(bf16[96,640]{1,0:T(8,128)(2,1)} %collective-permute-done.18), channel_id=1, source_target_pairs={{0,4},{4,8},{8,12},{12,14},{14,10},{10,6},{6,2},{2,0},{1,5},{5,9},... | collective-permute-start | bytes 368648 | tf_op jit(solution)/shard_map/ppermute | solution.py:173
  100.6 24.8 %collective-permute-start.6 = (bf16[768,640]{1,0:T(8,128)(2,1)S(1)}, bf16[768,640]{1,0:T(8,128)(2,1)}, u32[]{:S(2)}, u32[]{:S(2)}) collective-permute-start(bf16[768,640]{1,0:T(8,128)(2,1)S(1)} %gather_fusion.1), channel_id=1, source_target_pairs={{4,0},{8,4},{12,8},{14,12},{10,14},{6,10},{2,6},{0,2},{5,1},{9,5},... | collective-permute-start | bytes 2949128 | tf_op jit(solution)/shard_map/ppermute | solution.py:173
  102.4 7.1 %collective-permute-start.22 = (bf16[96,3456]{1,0:T(8,128)(2,1)S(1)}, bf16[96,3456]{1,0:T(8,128)(2,1)S(1)}, u32[]{:S(2)}, u32[]{:S(2)}) collective-permute-start(bf16[96,3456]{1,0:T(8,128)(2,1)S(1)} %copy-done), channel_id=1, source_target_pairs={{0,1},{1,0},{2,3},{3,2},{4,5},{5,4},{6,7},{7,6},{8,9},{9,8},{10,11... | collective-permute-start | bytes 1990664 | tf_op jit(solution)/shard_map/ppermute | solution.py:184
  109.5 16.1 %collective-permute-start.21 = (bf16[96,2560]{1,0:T(8,128)(2,1)S(1)}, bf16[96,2560]{1,0:T(8,128)(2,1)S(1)}, u32[]{:S(2)}, u32[]{:S(2)}) collective-permute-start(bf16[96,2560]{1,0:T(8,128)(2,1)S(1)} %pad_maximum_fusion), channel_id=1, source_target_pairs={{0,1},{1,0},{2,3},{3,2},{4,5},{5,4},{6,7},{7,6},{8,9},{9,8},{10,11... | collective-permute-start | bytes 1474568 | tf_op jit(solution)/shard_map/ppermute | solution.py:201
  110.3 61.1 %collective-permute-start.1 = (bf16[768,640]{1,0:T(8,128)(2,1)}, bf16[768,640]{1,0:T(8,128)(2,1)}, u32[]{:S(2)}, u32[]{:S(2)}) collective-permute-start(bf16[768,640]{1,0:T(8,128)(2,1)} %collective-permute-done.refs_1_), channel_id=1, source_target_pairs={{0,4},{4,8},{8,12},{12,14},{14,10},{10,6},{6,2},{2,0},{1,5},{5,9},... | collective-permute-start | bytes 2949128 | tf_op jit(solution)/shard_map/ppermute | solution.py:173
  112.1 59.3 %collective-permute-start.3 = (bf16[768,640]{1,0:T(8,128)(2,1)}, bf16[768,640]{1,0:T(8,128)(2,1)S(1)}, u32[]{:S(2)}, u32[]{:S(2)}) collective-permute-start(bf16[768,640]{1,0:T(8,128)(2,1)} %collective-permute-done.2.refs_2_), channel_id=1, source_target_pairs={{4,0},{8,4},{12,8},{14,12},{10,14},{6,10},{2,6},{0,2},{5,1},{9,5},... | collective-permute-start | bytes 2949128 | tf_op jit(solution)/shard_map/ppermute | solution.py:173
  112.4 59.1 %collective-permute-start.5 = (bf16[768,640]{1,0:T(8,128)(2,1)}, bf16[768,640]{1,0:T(8,128)(2,1)}, u32[]{:S(2)}, u32[]{:S(2)}) collective-permute-start(bf16[768,640]{1,0:T(8,128)(2,1)} %collective-permute-done.4.refs_4_), channel_id=1, source_target_pairs={{0,4},{4,8},{8,12},{12,14},{14,10},{10,6},{6,2},{2,0},{1,5},{5,9},... | collective-permute-start | bytes 2949128 | tf_op jit(solution)/shard_map/ppermute | solution.py:173
  125.4 46.1 %collective-permute-start.7 = (bf16[768,640]{1,0:T(8,128)(2,1)}, bf16[768,640]{1,0:T(8,128)(2,1)S(1)}, u32[]{:S(2)}, u32[]{:S(2)}) collective-permute-start(bf16[768,640]{1,0:T(8,128)(2,1)} %collective-permute-done.6.refs_5_), channel_id=1, source_target_pairs={{4,0},{8,4},{12,8},{14,12},{10,14},{6,10},{2,6},{0,2},{5,1},{9,5},... | collective-permute-start | bytes 2949128 | tf_op jit(solution)/shard_map/ppermute | solution.py:173
  171.5 31.3 %collective-permute-start.10 = (bf16[768,640]{1,0:T(8,128)(2,1)}, bf16[768,640]{1,0:T(8,128)(2,1)S(1)}, u32[]{:S(2)}, u32[]{:S(2)}) collective-permute-start(bf16[768,640]{1,0:T(8,128)(2,1)} %collective-permute-done.1.refs_0_), channel_id=1, source_target_pairs={{0,4},{4,8},{8,12},{12,14},{14,10},{10,6},{6,2},{2,0},{1,5},{5,9},... | collective-permute-start | bytes 2949128 | tf_op jit(solution)/shard_map/ppermute | solution.py:173
  173.3 29.5 %collective-permute-start.11 = (bf16[768,640]{1,0:T(8,128)(2,1)S(1)}, bf16[768,640]{1,0:T(8,128)(2,1)S(1)}, u32[]{:S(2)}, u32[]{:S(2)}) collective-permute-start(bf16[768,640]{1,0:T(8,128)(2,1)S(1)} %collective-permute-done.3.refs_1_), channel_id=1, source_target_pairs={{4,0},{8,4},{12,8},{14,12},{10,14},{6,10},{2,6},{0,2},{5,1},{9,5},... | collective-permute-start | bytes 2949128 | tf_op jit(solution)/shard_map/ppermute | solution.py:173
  173.5 41.1 %collective-permute-start.12 = (bf16[768,640]{1,0:T(8,128)(2,1)}, bf16[768,640]{1,0:T(8,128)(2,1)S(1)}, u32[]{:S(2)}, u32[]{:S(2)}) collective-permute-start(bf16[768,640]{1,0:T(8,128)(2,1)} %collective-permute-done.5.refs_2_), channel_id=1, source_target_pairs={{0,4},{4,8},{8,12},{12,14},{14,10},{10,6},{6,2},{2,0},{1,5},{5,9},... | collective-permute-start | bytes 2949128 | tf_op jit(solution)/shard_map/ppermute | solution.py:173
  175.3 39.6 %collective-permute-start.13 = (bf16[768,640]{1,0:T(8,128)(2,1)S(1)}, bf16[768,640]{1,0:T(8,128)(2,1)S(1)}, u32[]{:S(2)}, u32[]{:S(2)}) collective-permute-start(bf16[768,640]{1,0:T(8,128)(2,1)S(1)} %collective-permute-done.7.refs_3_), channel_id=1, source_target_pairs={{4,0},{8,4},{12,8},{14,12},{10,14},{6,10},{2,6},{0,2},{5,1},{9,5},... | collective-permute-start | bytes 2949128 | tf_op jit(solution)/shard_map/ppermute | solution.py:173
  215.0 29.3 %collective-permute-start.16 = (bf16[768,640]{1,0:T(8,128)(2,1)S(1)}, bf16[768,640]{1,0:T(8,128)(2,1)S(1)}, u32[]{:S(2)}, u32[]{:S(2)}) collective-permute-start(bf16[768,640]{1,0:T(8,128)(2,1)S(1)} %collective-permute-done.10.refs_0_), channel_id=1, source_target_pairs={{0,4},{4,8},{8,12},{12,14},{14,10},{10,6},{6,2},{2,0},{1,5},{5,9},... | collective-permute-start | bytes 2949128 | tf_op jit(solution)/shard_map/ppermute | solution.py:173
  216.6 27.8 %collective-permute-start.17 = (bf16[768,640]{1,0:T(8,128)(2,1)S(1)}, bf16[768,640]{1,0:T(8,128)(2,1)S(1)}, u32[]{:S(2)}, u32[]{:S(2)}) collective-permute-start(bf16[768,640]{1,0:T(8,128)(2,1)S(1)} %collective-permute-done.13.refs_3_), channel_id=1, source_target_pairs={{4,0},{8,4},{12,8},{14,12},{10,14},{6,10},{2,6},{0,2},{5,1},{9,5},... | collective-permute-start | bytes 2949128 | tf_op jit(solution)/shard_map/ppermute | solution.py:173
  (17 other events, 178.2 us)
Sparse Core Ops, SparseCore 0:
  9.6 58.1 all-gather.1
where the time goes:
time: 275 us; the launch traced here: 274 us
  Pallas kernels  111 us (40%)
  waiting for transfers between devices  55.7 us (20%)
  local copies, waits for them, and re-layouts  37 us (13%)
  between operations  29.6 us (11%)
  starting transfers between devices  24.2 us (9%)
  matrix products  10.1 us (4%)
  other arithmetic  6.5 us (2%)
    pallas_call x4, Pallas kernels, add_blocks(): pl.pallas_call(functools.partial(block_kernel, n_blocks, acc is not None,...  111 us
    ppermute x21, waiting for transfers between devices, send(): return lax.ppermute(x, 'out', perm)  55 us
    ppermute x21, starting transfers between devices, send(): return lax.ppermute(x, 'out', perm)  23.7 us
    gather x2, local copies, waits for them, and re-layouts, per_device(): top, bottom = (pool[ids[:half]], pool[ids[half:]])  14.2 us
    pad x8, local copies, waits for them, and re-layouts, blocks(): jnp.pad(a_of[s], pad)  10.8 us
    dot_general x1, matrix products, per_device(): lax.dot_general(a_pair, scaled, (((0,), (0,)), ((), ())), preferred_eleme...  10.1 us
    concatenate x3, other arithmetic, blocks(): jnp.concatenate([table[s + n // 2:s + n // 2 + 1] for s in shifts])  5.98 us
    unnamed x41, local copies, waits for them, and re-layouts  5.9 us
  transfers between devices with their start and end apart: 24, of which 6 were waited for; matrix products, arithmetic and copies ran while one was open for 19% of the time, Pallas kernels for 33%

commit v1 on v0

--- a/solution.py
+++ b/solution.py
@@ -177,10 +177,9 @@
     lanes = -(-mem_local // 128) * 128
     pad = ((0, lanes - mem_local), (0, 0))
     a_of = {0: factor_a}
-    for s in range(1, n // 2 + 1):
-        a_of[-s] = send(a_of[-(s - 1)], up)
-        if s < n // 2:
-            a_of[s] = send(a_of[s - 1], down)
+    for s in range(-(n // 2), n // 2):
+        if s != 0:
+            a_of[s] = send(factor_a, [(order[(k + s) % n], order[k]) for k in range(n)])
     b_other = lax.ppermute(factor_b, "inp", swap)
 
     ids = token_ids.reshape(-1)

time: 275 us -> 255 us (0.927)
  waiting for transfers between devices: 55.7 us -> 29.6 us
  starting transfers between devices: 24.2 us -> 30.3 us
    ppermute x21, waiting for transfers between devices: 55 us -> 27.7 us  [send(): return lax.ppermute(x, 'out', perm)]
    ppermute x21, starting transfers between devices: 23.7 us -> 29.7 us  [send(): return lax.ppermute(x, 'out', perm)]
    unnamed x41 -> x43, local copies, waits for them, and re-layouts: 5.9 us -> 6.03 us
  transfers between devices with their start and end apart: 24 -> 24, of which waited for: 6 -> 7; matrix products, arithmetic and copies ran while one was open for 19% -> 20% of each run, Pallas kernels for 33% -> 35%
where the time goes in v1:
time: 255 us; the launch traced here: 254 us
  Pallas kernels  111 us (44%)
  local copies, waits for them, and re-layouts  37.1 us (15%)
  starting transfers between devices  30.3 us (12%)
  waiting for transfers between devices  29.6 us (12%)
  between operations  29.5 us (12%)
  matrix products  10.1 us (4%)
  other arithmetic  6.74 us (3%)
    pallas_call x4, Pallas kernels, add_blocks(): pl.pallas_call(functools.partial(block_kernel, n_blocks, acc is not None,...  111 us
    ppermute x21, starting transfers between devices, send(): return lax.ppermute(x, 'out', perm)  29.7 us
    ppermute x21, waiting for transfers between devices, send(): return lax.ppermute(x, 'out', perm)  27.7 us
    gather x2, local copies, waits for them, and re-layouts, per_device(): top, bottom = (pool[ids[:half]], pool[ids[half:]])  14.1 us
    pad x8, local copies, waits for them, and re-layouts, blocks(): jnp.pad(a_of[s], pad)  10.9 us
    dot_general x1, matrix products, per_device(): lax.dot_general(a_pair, scaled, (((0,), (0,)), ((), ())), preferred_eleme...  10.1 us
    concatenate x3, other arithmetic, blocks(): jnp.concatenate([table[s + n // 2:s + n // 2 + 1] for s in shifts])  6.23 us
    unnamed x43, local copies, waits for them, and re-layouts  6.03 us
  transfers between devices with their start and end apart: 24, of which 7 were waited for; matrix products, arithmetic and copies ran while one was open for 20% of the time, Pallas kernels for 35%

profile of v1, /device:TPU:0, one launch (start us, length us, event | category | flops | bytes accessed | tf_op | source)
XLA Modules:
  0.0 254.1 jit_solution(11449736347360060965)
XLA Ops:
  8.1 3.0 %collective-permute-start.8 = (bf16[96,640]{1,0:T(8,128)(2,1)S(1)}, bf16[96,640]{1,0:T(8,128)(2,1)S(1)}, u32[]{:S(2)}, u32[]{:S(2)}) collective-permute-start(bf16[96,640]{1,0:T(8,128)(2,1)S(1)} %copy-done.13), channel_id=1, source_target_pairs={{2,0},{0,4},{4,8},{8,12},{12,14},{14,10},{10,6},{6,2},{3,1},{1,5},... | collective-permute-start | bytes 368648 | tf_op jit(solution)/shard_map/ppermute | solution.py:173
  11.1 3.0 %collective-permute-start.14 = (bf16[96,640]{1,0:T(8,128)(2,1)S(1)}, bf16[96,640]{1,0:T(8,128)(2,1)}, u32[]{:S(2)}, u32[]{:S(2)}) collective-permute-start(bf16[96,640]{1,0:T(8,128)(2,1)S(1)} %copy-done.13), channel_id=1, source_target_pairs={{6,0},{2,4},{0,8},{4,12},{8,14},{12,10},{14,6},{10,2},{7,1},{3,5},... | collective-permute-start | bytes 368648 | tf_op jit(solution)/shard_map/ppermute | solution.py:173
  14.1 4.9 %collective-permute-start.18 = (bf16[96,640]{1,0:T(8,128)(2,1)S(1)}, bf16[96,640]{1,0:T(8,128)(2,1)}, u32[]{:S(2)}, u32[]{:S(2)}) collective-permute-start(bf16[96,640]{1,0:T(8,128)(2,1)S(1)} %copy-done.13), channel_id=1, source_target_pairs={{14,0},{10,4},{6,8},{2,12},{0,14},{4,10},{8,6},{12,2},{15,1},{11,5... | collective-permute-start | bytes 368648 | tf_op jit(solution)/shard_map/ppermute | solution.py:173
  22.0 1.9 pad_add_fusion.1.own_ref
  24.8 3.6 %collective-permute-start.20 = (bf16[96,640]{1,0:T(8,128)(2,1)S(1)}, bf16[96,640]{1,0:T(8,128)(2,1)}, u32[]{:S(2)}, u32[]{:S(2)}) collective-permute-start(bf16[96,640]{1,0:T(8,128)(2,1)S(1)} %copy-done.13), channel_id=1, source_target_pairs={{12,0},{14,4},{10,8},{6,12},{2,14},{0,10},{4,6},{8,2},{13,1},{15,5... | collective-permute-start | bytes 368648 | tf_op jit(solution)/shard_map/ppermute | solution.py:173
  28.5 1.9 pad_add_fusion.2.own_ref
  42.1 7.6 %gather_fusion = bf16[768,640]{1,0:T(8,128)(2,1)S(1)} fusion(bf16[4096,640]{1,0:T(8,128)(2,1)} %param.7, s32[1024]{0:T(1024)S(1)} %pad_clamp_fusion.1), kind=kCustom, calls=%fused_computation | custom fusion | bytes 1969152 | tf_op jit(solution)/shard_map/gather | solution.py:186
  49.8 6.4 %gather_fusion.1 = bf16[768,640]{1,0:T(8,128)(2,1)S(1)} fusion(bf16[4096,640]{1,0:T(8,128)(2,1)} %param.7, s32[1024]{0:T(1024)S(1)} %pad_clamp_fusion), kind=kCustom, calls=%fused_computation.1 | custom fusion | bytes 1969152 | tf_op jit(solution)/shard_map/gather | solution.py:186
  61.3 2.4 pad_add_fusion.own_ref
  67.6 2.0 collective-permute-start.2
  69.6 1.6 pad.33.refs_5_
  72.8 2.0 collective-permute-start.6
  76.4 1.6 pad.36.refs_5_
  86.4 10.1 %convolution_convert_fusion = bf16[2560,3456]{1,0:T(8,128)(2,1)} fusion(bf16[96,3456]{1,0:T(8,128)(2,1)S(1)} %multiply_convert_fusion, bf16[96,3456]{1,0:T(8,128)(2,1)S(1)} %multiply_convert_fusion.1, bf16[96,2560]{1,0:T(8,128)(2,1)} %copy-done.12, bf16[96,640]{1,0:T(8,128)(2,1)S(1)} %get-tuple-element.43, bf16[96,640]{1,0:T(8,128)(2,1)} %get-tuple-element.44, ...), kind=kOutput, calls=%fused_computation.2 | convolution fusion | flops 3413803008 | bytes 20004864 | tf_op jit(solution)/shard_map/dot_general | solution.py:210
  96.6 2.0 collective-permute-start.3
  98.6 13.3 %collective-permute-done.4.refs_4_ = bf16[768,640]{1,0:T(8,128)(2,1)} collective-permute-done((bf16[768,640]{1,0:T(8,128)(2,1)S(1)}, bf16[768,640]{1,0:T(8,128)(2,1)}, u32[]{:S(2)}, u32[]{:S(2)}) %collective-permute-start.4) | collective-permute-done | bytes 983072 | tf_op jit(solution)/shard_map/ppermute | solution.py:173
  111.8 1.6 collective-permute-done.6.refs_5_
  113.4 2.0 collective-permute-start.7
  115.4 34.8 %shard_map.86 = (f32[1536,3456]{1,0:T(8,128)}, f32[1536,128]{1,0:T(8,128)}) custom-call(s32[3]{0:T(128)} %pad_add_fusion.own_ref, bf16[768,640]{1,0:T(8,128)(2,1)} %copy-done.1, bf16[768,640]{1,0:T(8,128)(2,1)} %collective-permute-done.refs_1_, bf16[768,640]{1,0:T(8,128)(2,1)} %collective-permute-done.2.refs_2_, bf16[768,640]{1,0:T(8,128)(2,1)} %copy-done.2, ...), custom_call_target="tpu_custom_call" | custom-call | flops 20384317440 | bytes 40402944 | tf_op jit(solution)/shard_map/pallas_call | solution.py:133
  156.3 27.3 %shard_map.87 = (f32[1536,3456]{1,0:T(8,128)}, f32[1536,128]{1,0:T(8,128)}) custom-call(s32[2]{0:T(128)} %pad_add_fusion.1.own_ref, bf16[768,640]{1,0:T(8,128)(2,1)} %copy-done.3, bf16[768,640]{1,0:T(8,128)(2,1)} %copy-done.4, bf16[768,640]{1,0:T(8,128)(2,1)} %collective-permute-done.5.refs_2_, bf16[768,640]{1,0:T(8,128)(2,1)} %copy-done.5, ...), custom_call_target="tpu_custom_call" | custom-call | flops 13589544960 | bytes 55246848 | tf_op jit(solution)/shard_map/pallas_call | solution.py:133
  183.7 10.6 %collective-permute-done.12.refs_2_ = bf16[768,640]{1,0:T(8,128)(2,1)S(1)} collective-permute-done((bf16[768,640]{1,0:T(8,128)(2,1)}, bf16[768,640]{1,0:T(8,128)(2,1)S(1)}, u32[]{:S(2)}, u32[]{:S(2)}) %collective-permute-start.12) | collective-permute-done | bytes 983072 | tf_op jit(solution)/shard_map/ppermute | solution.py:173
  194.7 2.5 collective-permute-start.16
  197.2 27.2 %shard_map.88 = (f32[1536,3456]{1,0:T(8,128)}, f32[1536,128]{1,0:T(8,128)}) custom-call(s32[2]{0:T(128)} %pad_add_fusion.2.own_ref, bf16[768,640]{1,0:T(8,128)(2,1)} %copy-done.6, bf16[768,640]{1,0:T(8,128)(2,1)} %copy-done.7, bf16[768,640]{1,0:T(8,128)(2,1)} %copy-done.9, bf16[768,640]{1,0:T(8,128)(2,1)} %copy-done.8, bf16[128,640]{1,0:T(8,128)(2,1)} %pad.35.refs_4_, ...), custom_call_target="tpu_custom_call" | custom-call | flops 13589544960 | bytes 55246848 | tf_op jit(solution)/shard_map/pallas_call | solution.py:133
  225.8 21.4 %shard_map.89 = bf16[1536,3456]{1,0:T(8,128)(2,1)} custom-call(s32[1]{0:T(128)} %bitcast.own_ref, bf16[768,640]{1,0:T(8,128)(2,1)} %copy-done.10, bf16[768,640]{1,0:T(8,128)(2,1)} %copy-done.11, bf16[128,640]{1,0:T(8,128)(2,1)} %pad.34.refs_2_, bf16[5120,3456]{1,0:T(8,128)(2,1)} %all-gather.2.cloned.1.call-done.refs_9_.refs_6_.refs_3_, ...), custom_call_target="tpu_custom_call" | custom-call | flops 9512681472 | bytes 38240256 | tf_op jit(solution)/shard_map/pallas_call | solution.py:133
  (106 shorter events, 29.7 us)
Async XLA Ops:
  7.2 108.2 %all-gather.2.cloned.1.call-start = ((), (), s32[]{:S(2)}) async-start(), calls=%async_computation | async-start | bytes 53084160 | tf_op jit(solution)/shard_map/all_gather | solution.py:187
  8.1 16.5 %collective-permute-start.8 = (bf16[96,640]{1,0:T(8,128)(2,1)S(1)}, bf16[96,640]{1,0:T(8,128)(2,1)S(1)}, u32[]{:S(2)}, u32[]{:S(2)}) collective-permute-start(bf16[96,640]{1,0:T(8,128)(2,1)S(1)} %copy-done.13), channel_id=1, source_target_pairs={{2,0},{0,4},{4,8},{8,12},{12,14},{14,10},{10,6},{6,2},{3,1},{1,5},... | collective-permute-start | bytes 368648 | tf_op jit(solution)/shard_map/ppermute | solution.py:173
  11.1 13.8 %collective-permute-start.9 = (bf16[96,640]{1,0:T(8,128)(2,1)S(1)}, bf16[96,640]{1,0:T(8,128)(2,1)S(1)}, u32[]{:S(2)}, u32[]{:S(2)}) collective-permute-start(bf16[96,640]{1,0:T(8,128)(2,1)S(1)} %copy-done.13), channel_id=1, source_target_pairs={{4,0},{8,4},{12,8},{14,12},{10,14},{6,10},{2,6},{0,2},{5,1},{9,5},... | collective-permute-start | bytes 368648 | tf_op jit(solution)/shard_map/ppermute | solution.py:173
  11.1 54.9 %collective-permute-start.14 = (bf16[96,640]{1,0:T(8,128)(2,1)S(1)}, bf16[96,640]{1,0:T(8,128)(2,1)}, u32[]{:S(2)}, u32[]{:S(2)}) collective-permute-start(bf16[96,640]{1,0:T(8,128)(2,1)S(1)} %copy-done.13), channel_id=1, source_target_pairs={{6,0},{2,4},{0,8},{4,12},{8,14},{12,10},{14,6},{10,2},{7,1},{3,5},... | collective-permute-start | bytes 368648 | tf_op jit(solution)/shard_map/ppermute | solution.py:173
  14.1 53.4 %collective-permute-start.15 = (bf16[96,640]{1,0:T(8,128)(2,1)S(1)}, bf16[96,640]{1,0:T(8,128)(2,1)}, u32[]{:S(2)}, u32[]{:S(2)}) collective-permute-start(bf16[96,640]{1,0:T(8,128)(2,1)S(1)} %copy-done.13), channel_id=1, source_target_pairs={{8,0},{12,4},{14,8},{10,12},{6,14},{2,10},{0,6},{4,2},{9,1},{13,5}... | collective-permute-start | bytes 368648 | tf_op jit(solution)/shard_map/ppermute | solution.py:173
  14.1 57.0 %collective-permute-start.18 = (bf16[96,640]{1,0:T(8,128)(2,1)S(1)}, bf16[96,640]{1,0:T(8,128)(2,1)}, u32[]{:S(2)}, u32[]{:S(2)}) collective-permute-start(bf16[96,640]{1,0:T(8,128)(2,1)S(1)} %copy-done.13), channel_id=1, source_target_pairs={{14,0},{10,4},{6,8},{2,12},{0,14},{4,10},{8,6},{12,2},{15,1},{11,5... | collective-permute-start | bytes 368648 | tf_op jit(solution)/shard_map/ppermute | solution.py:173
  24.6 48.2 %collective-permute-start.19 = (bf16[96,640]{1,0:T(8,128)(2,1)S(1)}, bf16[96,640]{1,0:T(8,128)(2,1)}, u32[]{:S(2)}, u32[]{:S(2)}) collective-permute-start(bf16[96,640]{1,0:T(8,128)(2,1)S(1)} %copy-done.13), channel_id=1, source_target_pairs={{10,0},{6,4},{2,8},{0,12},{4,14},{8,10},{12,6},{14,2},{11,1},{7,5}... | collective-permute-start | bytes 368648 | tf_op jit(solution)/shard_map/ppermute | solution.py:173
  24.8 51.5 %collective-permute-start.20 = (bf16[96,640]{1,0:T(8,128)(2,1)S(1)}, bf16[96,640]{1,0:T(8,128)(2,1)}, u32[]{:S(2)}, u32[]{:S(2)}) collective-permute-start(bf16[96,640]{1,0:T(8,128)(2,1)S(1)} %copy-done.13), channel_id=1, source_target_pairs={{12,0},{14,4},{10,8},{6,12},{2,14},{0,10},{4,6},{8,2},{13,1},{15,5... | collective-permute-start | bytes 368648 | tf_op jit(solution)/shard_map/ppermute | solution.py:173
  66.0 30.6 %collective-permute-start = (bf16[768,640]{1,0:T(8,128)(2,1)S(1)}, bf16[768,640]{1,0:T(8,128)(2,1)}, u32[]{:S(2)}, u32[]{:S(2)}) collective-permute-start(bf16[768,640]{1,0:T(8,128)(2,1)S(1)} %gather_fusion), channel_id=1, source_target_pairs={{0,4},{4,8},{8,12},{12,14},{14,10},{10,6},{6,2},{2,0},{1,5},{5,9},... | collective-permute-start | bytes 2949128 | tf_op jit(solution)/shard_map/ppermute | solution.py:173
  67.6 29.0 %collective-permute-start.2 = (bf16[768,640]{1,0:T(8,128)(2,1)S(1)}, bf16[768,640]{1,0:T(8,128)(2,1)}, u32[]{:S(2)}, u32[]{:S(2)}) collective-permute-start(bf16[768,640]{1,0:T(8,128)(2,1)S(1)} %gather_fusion), channel_id=1, source_target_pairs={{4,0},{8,4},{12,8},{14,12},{10,14},{6,10},{2,6},{0,2},{5,1},{9,5},... | collective-permute-start | bytes 2949128 | tf_op jit(solution)/shard_map/ppermute | solution.py:173
  71.2 40.7 %collective-permute-start.4 = (bf16[768,640]{1,0:T(8,128)(2,1)S(1)}, bf16[768,640]{1,0:T(8,128)(2,1)}, u32[]{:S(2)}, u32[]{:S(2)}) collective-permute-start(bf16[768,640]{1,0:T(8,128)(2,1)S(1)} %gather_fusion.1), channel_id=1, source_target_pairs={{0,4},{4,8},{8,12},{12,14},{14,10},{10,6},{6,2},{2,0},{1,5},{5,9},... | collective-permute-start | bytes 2949128 | tf_op jit(solution)/shard_map/ppermute | solution.py:173
  72.8 40.7 %collective-permute-start.6 = (bf16[768,640]{1,0:T(8,128)(2,1)S(1)}, bf16[768,640]{1,0:T(8,128)(2,1)}, u32[]{:S(2)}, u32[]{:S(2)}) collective-permute-start(bf16[768,640]{1,0:T(8,128)(2,1)S(1)} %gather_fusion.1), channel_id=1, source_target_pairs={{4,0},{8,4},{12,8},{14,12},{10,14},{6,10},{2,6},{0,2},{5,1},{9,5},... | collective-permute-start | bytes 2949128 | tf_op jit(solution)/shard_map/ppermute | solution.py:173
  76.4 7.2 %collective-permute-start.22 = (bf16[96,3456]{1,0:T(8,128)(2,1)S(1)}, bf16[96,3456]{1,0:T(8,128)(2,1)S(1)}, u32[]{:S(2)}, u32[]{:S(2)}) collective-permute-start(bf16[96,3456]{1,0:T(8,128)(2,1)S(1)} %copy-done), channel_id=1, source_target_pairs={{0,1},{1,0},{2,3},{3,2},{4,5},{5,4},{6,7},{7,6},{8,9},{9,8},{10,11... | collective-permute-start | bytes 1990664 | tf_op jit(solution)/shard_map/ppermute | solution.py:183
  83.6 2.1 collective-permute-start.21
  96.5 53.8 %collective-permute-start.1 = (bf16[768,640]{1,0:T(8,128)(2,1)}, bf16[768,640]{1,0:T(8,128)(2,1)S(1)}, u32[]{:S(2)}, u32[]{:S(2)}) collective-permute-start(bf16[768,640]{1,0:T(8,128)(2,1)} %collective-permute-done.refs_1_), channel_id=1, source_target_pairs={{0,4},{4,8},{8,12},{12,14},{14,10},{10,6},{6,2},{2,0},{1,5},{5,9},... | collective-permute-start | bytes 2949128 | tf_op jit(solution)/shard_map/ppermute | solution.py:173
  96.6 53.8 %collective-permute-start.3 = (bf16[768,640]{1,0:T(8,128)(2,1)}, bf16[768,640]{1,0:T(8,128)(2,1)S(1)}, u32[]{:S(2)}, u32[]{:S(2)}) collective-permute-start(bf16[768,640]{1,0:T(8,128)(2,1)} %collective-permute-done.2.refs_2_), channel_id=1, source_target_pairs={{4,0},{8,4},{12,8},{14,12},{10,14},{6,10},{2,6},{0,2},{5,1},{9,5},... | collective-permute-start | bytes 2949128 | tf_op jit(solution)/shard_map/ppermute | solution.py:173
  111.8 38.8 %collective-permute-start.5 = (bf16[768,640]{1,0:T(8,128)(2,1)}, bf16[768,640]{1,0:T(8,128)(2,1)}, u32[]{:S(2)}, u32[]{:S(2)}) collective-permute-start(bf16[768,640]{1,0:T(8,128)(2,1)} %collective-permute-done.4.refs_4_), channel_id=1, source_target_pairs={{0,4},{4,8},{8,12},{12,14},{14,10},{10,6},{6,2},{2,0},{1,5},{5,9},... | collective-permute-start | bytes 2949128 | tf_op jit(solution)/shard_map/ppermute | solution.py:173
  113.4 38.7 %collective-permute-start.7 = (bf16[768,640]{1,0:T(8,128)(2,1)}, bf16[768,640]{1,0:T(8,128)(2,1)S(1)}, u32[]{:S(2)}, u32[]{:S(2)}) collective-permute-start(bf16[768,640]{1,0:T(8,128)(2,1)} %collective-permute-done.6.refs_5_), channel_id=1, source_target_pairs={{4,0},{8,4},{12,8},{14,12},{10,14},{6,10},{2,6},{0,2},{5,1},{9,5},... | collective-permute-start | bytes 2949128 | tf_op jit(solution)/shard_map/ppermute | solution.py:173
  152.1 31.5 %collective-permute-start.10 = (bf16[768,640]{1,0:T(8,128)(2,1)S(1)}, bf16[768,640]{1,0:T(8,128)(2,1)S(1)}, u32[]{:S(2)}, u32[]{:S(2)}) collective-permute-start(bf16[768,640]{1,0:T(8,128)(2,1)S(1)} %collective-permute-done.1.refs_0_), channel_id=1, source_target_pairs={{0,4},{4,8},{8,12},{12,14},{14,10},{10,6},{6,2},{2,0},{1,5},{5,9},... | collective-permute-start | bytes 2949128 | tf_op jit(solution)/shard_map/ppermute | solution.py:173
  153.0 30.6 %collective-permute-start.11 = (bf16[768,640]{1,0:T(8,128)(2,1)S(1)}, bf16[768,640]{1,0:T(8,128)(2,1)S(1)}, u32[]{:S(2)}, u32[]{:S(2)}) collective-permute-start(bf16[768,640]{1,0:T(8,128)(2,1)S(1)} %collective-permute-done.3.refs_1_), channel_id=1, source_target_pairs={{4,0},{8,4},{12,8},{14,12},{10,14},{6,10},{2,6},{0,2},{5,1},{9,5},... | collective-permute-start | bytes 2949128 | tf_op jit(solution)/shard_map/ppermute | solution.py:173
  154.3 39.9 %collective-permute-start.12 = (bf16[768,640]{1,0:T(8,128)(2,1)}, bf16[768,640]{1,0:T(8,128)(2,1)S(1)}, u32[]{:S(2)}, u32[]{:S(2)}) collective-permute-start(bf16[768,640]{1,0:T(8,128)(2,1)} %collective-permute-done.5.refs_2_), channel_id=1, source_target_pairs={{0,4},{4,8},{8,12},{12,14},{14,10},{10,6},{6,2},{2,0},{1,5},{5,9},... | collective-permute-start | bytes 2949128 | tf_op jit(solution)/shard_map/ppermute | solution.py:173
  155.0 39.6 %collective-permute-start.13 = (bf16[768,640]{1,0:T(8,128)(2,1)S(1)}, bf16[768,640]{1,0:T(8,128)(2,1)S(1)}, u32[]{:S(2)}, u32[]{:S(2)}) collective-permute-start(bf16[768,640]{1,0:T(8,128)(2,1)S(1)} %collective-permute-done.7.refs_3_), channel_id=1, source_target_pairs={{4,0},{8,4},{12,8},{14,12},{10,14},{6,10},{2,6},{0,2},{5,1},{9,5},... | collective-permute-start | bytes 2949128 | tf_op jit(solution)/shard_map/ppermute | solution.py:173
  194.7 29.8 %collective-permute-start.16 = (bf16[768,640]{1,0:T(8,128)(2,1)S(1)}, bf16[768,640]{1,0:T(8,128)(2,1)S(1)}, u32[]{:S(2)}, u32[]{:S(2)}) collective-permute-start(bf16[768,640]{1,0:T(8,128)(2,1)S(1)} %collective-permute-done.10.refs_0_), channel_id=1, source_target_pairs={{0,4},{4,8},{8,12},{12,14},{14,10},{10,6},{6,2},{2,0},{1,5},{5,9},... | collective-permute-start | bytes 2949128 | tf_op jit(solution)/shard_map/ppermute | solution.py:173
  197.2 27.3 %collective-permute-start.17 = (bf16[768,640]{1,0:T(8,128)(2,1)S(1)}, bf16[768,640]{1,0:T(8,128)(2,1)S(1)}, u32[]{:S(2)}, u32[]{:S(2)}) collective-permute-start(bf16[768,640]{1,0:T(8,128)(2,1)S(1)} %collective-permute-done.13.refs_3_), channel_id=1, source_target_pairs={{4,0},{8,4},{12,8},{14,12},{10,14},{6,10},{2,6},{0,2},{5,1},{9,5},... | collective-permute-start | bytes 2949128 | tf_op jit(solution)/shard_map/ppermute | solution.py:173
  (18 other events, 173.3 us)
Sparse Core Ops, SparseCore 0:
  9.6 58.1 all-gather.1

commit v2 on v1

--- a/solution.py
+++ b/solution.py
@@ -174,16 +174,17 @@
 
     swap = [(0, 1), (1, 0)]
 
+    b_other = lax.ppermute(factor_b, "inp", swap)
+
+    ids = token_ids.reshape(-1)
+    top, bottom = pool[ids[:half]], pool[ids[half:]]
     lanes = -(-mem_local // 128) * 128
     pad = ((0, lanes - mem_local), (0, 0))
+    a_sent, top, bottom = lax.optimization_barrier((factor_a, top, bottom))
     a_of = {0: factor_a}
     for s in range(-(n // 2), n // 2):
         if s != 0:
-            a_of[s] = send(factor_a, [(order[(k + s) % n], order[k]) for k in range(n)])
-    b_other = lax.ppermute(factor_b, "inp", swap)
-
-    ids = token_ids.reshape(-1)
-    top, bottom = pool[ids[:half]], pool[ids[half:]]
+            a_of[s] = send(a_sent, [(order[(k + s) % n], order[k]) for k in range(n)])
     w_all = lax.all_gather(weight, "inp", axis=0, tiled=True)
 
     stacked = jnp.stack([a_of[s] for s in range(-(n // 2), n // 2)])

time: 255 us -> 254 us (level)
    unnamed x43 -> x37, local copies, waits for them, and re-layouts: 6.03 us -> 6.01 us
where the time goes in v2:
time: 254 us; the launch traced here: 253 us
  Pallas kernels  111 us (44%)
  local copies, waits for them, and re-layouts  35.5 us (14%)
  waiting for transfers between devices  30.6 us (12%)
  starting transfers between devices  30.2 us (12%)
  between operations  29 us (11%)
  matrix products  10.1 us (4%)
  other arithmetic  6.53 us (3%)
    pallas_call x4, Pallas kernels, add_blocks(): pl.pallas_call(functools.partial(block_kernel, n_blocks, acc is not None,...  111 us
    ppermute x21, starting transfers between devices, send(): return lax.ppermute(x, 'out', perm)  29.6 us
    ppermute x21, waiting for transfers between devices, send(): return lax.ppermute(x, 'out', perm)  28.6 us
    gather x2, local copies, waits for them, and re-layouts, per_device(): top, bottom = (pool[ids[:half]], pool[ids[half:]])  12.6 us
    pad x8, local copies, waits for them, and re-layouts, blocks(): jnp.pad(a_of[s], pad)  10.8 us
    dot_general x1, matrix products, per_device(): lax.dot_general(a_pair, scaled, (((0,), (0,)), ((), ())), preferred_eleme...  10.1 us
    unnamed x37, local copies, waits for them, and re-layouts  6.01 us
    concatenate x3, other arithmetic, blocks(): jnp.concatenate([table[s + n // 2:s + n // 2 + 1] for s in shifts])  6.01 us
  transfers between devices with their start and end apart: 24, of which 7 were waited for; matrix products, arithmetic and copies ran while one was open for 20% of the time, Pallas kernels for 35%

profile of v2, /device:TPU:0, one launch (start us, length us, event | category | flops | bytes accessed | tf_op | source)
XLA Modules:
  0.0 252.9 jit_solution(16202517269049345227)
XLA Ops:
  8.4 6.1 %gather_fusion = bf16[768,640]{1,0:T(8,128)(2,1)S(1)} fusion(bf16[4096,640]{1,0:T(8,128)(2,1)} %param.7, s32[1024]{0:T(1024)S(1)} %pad_clamp_fusion.1), kind=kCustom, calls=%fused_computation | custom fusion | bytes 1969152 | tf_op jit(solution)/shard_map/gather | solution.py:180
  14.5 6.5 %gather_fusion.1 = bf16[768,640]{1,0:T(8,128)(2,1)S(1)} fusion(bf16[4096,640]{1,0:T(8,128)(2,1)} %param.7, s32[1024]{0:T(1024)S(1)} %pad_clamp_fusion), kind=kCustom, calls=%fused_computation.1 | custom fusion | bytes 1969152 | tf_op jit(solution)/shard_map/gather | solution.py:180
  21.1 3.5 %collective-permute-start.8 = (bf16[96,640]{1,0:T(8,128)(2,1)S(1)}, bf16[96,640]{1,0:T(8,128)(2,1)}, u32[]{:S(2)}, u32[]{:S(2)}) collective-permute-start(bf16[96,640]{1,0:T(8,128)(2,1)S(1)} %copy-done.12), channel_id=1, source_target_pairs={{2,0},{0,4},{4,8},{8,12},{12,14},{14,10},{10,6},{6,2},{3,1},{1,5},... | collective-permute-start | bytes 368648 | tf_op jit(solution)/shard_map/ppermute | solution.py:173
  24.5 3.1 %collective-permute-start.14 = (bf16[96,640]{1,0:T(8,128)(2,1)S(1)}, bf16[96,640]{1,0:T(8,128)(2,1)}, u32[]{:S(2)}, u32[]{:S(2)}) collective-permute-start(bf16[96,640]{1,0:T(8,128)(2,1)S(1)} %copy-done.12), channel_id=1, source_target_pairs={{6,0},{2,4},{0,8},{4,12},{8,14},{12,10},{14,6},{10,2},{7,1},{3,5},... | collective-permute-start | bytes 368648 | tf_op jit(solution)/shard_map/ppermute | solution.py:173
  27.7 5.0 %collective-permute-start.18 = (bf16[96,640]{1,0:T(8,128)(2,1)S(1)}, bf16[96,640]{1,0:T(8,128)(2,1)}, u32[]{:S(2)}, u32[]{:S(2)}) collective-permute-start(bf16[96,640]{1,0:T(8,128)(2,1)S(1)} %copy-done.12), channel_id=1, source_target_pairs={{14,0},{10,4},{6,8},{2,12},{0,14},{4,10},{8,6},{12,2},{15,1},{11,5... | collective-permute-start | bytes 368648 | tf_op jit(solution)/shard_map/ppermute | solution.py:173
  35.1 1.9 pad_add_fusion.1.own_ref
  37.7 3.8 %collective-permute-start.20 = (bf16[96,640]{1,0:T(8,128)(2,1)S(1)}, bf16[96,640]{1,0:T(8,128)(2,1)}, u32[]{:S(2)}, u32[]{:S(2)}) collective-permute-start(bf16[96,640]{1,0:T(8,128)(2,1)S(1)} %copy-done.12), channel_id=1, source_target_pairs={{12,0},{14,4},{10,8},{6,12},{2,14},{0,10},{4,6},{8,2},{13,1},{15,5... | collective-permute-start | bytes 368648 | tf_op jit(solution)/shard_map/ppermute | solution.py:173
  41.5 1.8 pad_add_fusion.2.own_ref
  59.7 2.3 pad_add_fusion.own_ref
  65.8 2.0 collective-permute-start.2
  71.0 2.0 collective-permute-start.6
  84.9 10.1 %convolution_convert_fusion = bf16[2560,3456]{1,0:T(8,128)(2,1)} fusion(bf16[96,3456]{1,0:T(8,128)(2,1)S(1)} %multiply_convert_fusion, bf16[96,3456]{1,0:T(8,128)(2,1)S(1)} %multiply_convert_fusion.1, bf16[96,2560]{1,0:T(8,128)(2,1)} %collective-permute-done.21, bf16[96,640]{1,0:T(8,128)(2,1)S(1)} %get-tuple-element.49, ...), kind=kOutput, calls=%fused_computation.2 | convolution fusion | flops 3413803008 | bytes 20004864 | tf_op jit(solution)/shard_map/dot_general | solution.py:211
  95.0 2.0 collective-permute-start.3
  97.0 13.1 %collective-permute-done.4.refs_4_ = bf16[768,640]{1,0:T(8,128)(2,1)} collective-permute-done((bf16[768,640]{1,0:T(8,128)(2,1)S(1)}, bf16[768,640]{1,0:T(8,128)(2,1)}, u32[]{:S(2)}, u32[]{:S(2)}) %collective-permute-start.4) | collective-permute-done | bytes 983072 | tf_op jit(solution)/shard_map/ppermute | solution.py:173
  111.7 2.0 collective-permute-start.7
  113.7 34.8 %shard_map.86 = (f32[1536,3456]{1,0:T(8,128)}, f32[1536,128]{1,0:T(8,128)}) custom-call(s32[3]{0:T(128)} %pad_add_fusion.own_ref, bf16[768,640]{1,0:T(8,128)(2,1)} %copy-done.1, bf16[768,640]{1,0:T(8,128)(2,1)} %collective-permute-done.refs_1_, bf16[768,640]{1,0:T(8,128)(2,1)} %collective-permute-done.2.refs_2_, bf16[768,640]{1,0:T(8,128)(2,1)} %copy-done.2, ...), custom_call_target="tpu_custom_call" | custom-call | flops 20384317440 | bytes 40402944 | tf_op jit(solution)/shard_map/pallas_call | solution.py:133
  148.8 2.0 collective-permute-done.7.refs_3_
  150.8 2.0 collective-permute-start.11
  152.9 2.0 collective-permute-start.13
  154.9 27.3 %shard_map.87 = (f32[1536,3456]{1,0:T(8,128)}, f32[1536,128]{1,0:T(8,128)}) custom-call(s32[2]{0:T(128)} %pad_add_fusion.1.own_ref, bf16[768,640]{1,0:T(8,128)(2,1)} %copy-done.3, bf16[768,640]{1,0:T(8,128)(2,1)} %copy-done.4, bf16[768,640]{1,0:T(8,128)(2,1)} %collective-permute-done.5.refs_2_, bf16[768,640]{1,0:T(8,128)(2,1)} %copy-done.5, ...), custom_call_target="tpu_custom_call" | custom-call | flops 13589544960 | bytes 55246848 | tf_op jit(solution)/shard_map/pallas_call | solution.py:133
  182.2 10.4 %collective-permute-done.12.refs_2_ = bf16[768,640]{1,0:T(8,128)(2,1)S(1)} collective-permute-done((bf16[768,640]{1,0:T(8,128)(2,1)}, bf16[768,640]{1,0:T(8,128)(2,1)S(1)}, u32[]{:S(2)}, u32[]{:S(2)}) %collective-permute-start.12) | collective-permute-done | bytes 983072 | tf_op jit(solution)/shard_map/ppermute | solution.py:173
  193.8 2.0 collective-permute-start.17
  195.9 27.2 %shard_map.88 = (f32[1536,3456]{1,0:T(8,128)}, f32[1536,128]{1,0:T(8,128)}) custom-call(s32[2]{0:T(128)} %pad_add_fusion.2.own_ref, bf16[768,640]{1,0:T(8,128)(2,1)} %copy-done.6, bf16[768,640]{1,0:T(8,128)(2,1)} %copy-done.7, bf16[768,640]{1,0:T(8,128)(2,1)} %copy-done.9, bf16[768,640]{1,0:T(8,128)(2,1)} %copy-done.8, bf16[128,640]{1,0:T(8,128)(2,1)} %pad.35.refs_4_, ...), custom_call_target="tpu_custom_call" | custom-call | flops 13589544960 | bytes 55246848 | tf_op jit(solution)/shard_map/pallas_call | solution.py:133
  224.5 21.5 %shard_map.89 = bf16[1536,3456]{1,0:T(8,128)(2,1)} custom-call(s32[1]{0:T(128)} %bitcast.own_ref, bf16[768,640]{1,0:T(8,128)(2,1)} %copy-done.10, bf16[768,640]{1,0:T(8,128)(2,1)} %copy-done.11, bf16[128,640]{1,0:T(8,128)(2,1)} %pad.34.refs_2_, bf16[5120,3456]{1,0:T(8,128)(2,1)} %all-gather.2.cloned.1.call-done.refs_9_.refs_6_.refs_3_, ...), custom_call_target="tpu_custom_call" | custom-call | flops 9512681472 | bytes 38240256 | tf_op jit(solution)/shard_map/pallas_call | solution.py:133
  (100 shorter events, 29.3 us)
Async XLA Ops:
  7.2 106.5 %all-gather.2.cloned.1.call-start = ((), (), s32[]{:S(2)}) async-start(), calls=%async_computation | async-start | bytes 53084160 | tf_op jit(solution)/shard_map/all_gather | solution.py:188
  21.1 16.6 %collective-permute-start.8 = (bf16[96,640]{1,0:T(8,128)(2,1)S(1)}, bf16[96,640]{1,0:T(8,128)(2,1)}, u32[]{:S(2)}, u32[]{:S(2)}) collective-permute-start(bf16[96,640]{1,0:T(8,128)(2,1)S(1)} %copy-done.12), channel_id=1, source_target_pairs={{2,0},{0,4},{4,8},{8,12},{12,14},{14,10},{10,6},{6,2},{3,1},{1,5},... | collective-permute-start | bytes 368648 | tf_op jit(solution)/shard_map/ppermute | solution.py:173
  24.5 13.2 %collective-permute-start.9 = (bf16[96,640]{1,0:T(8,128)(2,1)S(1)}, bf16[96,640]{1,0:T(8,128)(2,1)S(1)}, u32[]{:S(2)}, u32[]{:S(2)}) collective-permute-start(bf16[96,640]{1,0:T(8,128)(2,1)S(1)} %copy-done.12), channel_id=1, source_target_pairs={{4,0},{8,4},{12,8},{14,12},{10,14},{6,10},{2,6},{0,2},{5,1},{9,5},... | collective-permute-start | bytes 368648 | tf_op jit(solution)/shard_map/ppermute | solution.py:173
  24.5 39.7 %collective-permute-start.14 = (bf16[96,640]{1,0:T(8,128)(2,1)S(1)}, bf16[96,640]{1,0:T(8,128)(2,1)}, u32[]{:S(2)}, u32[]{:S(2)}) collective-permute-start(bf16[96,640]{1,0:T(8,128)(2,1)S(1)} %copy-done.12), channel_id=1, source_target_pairs={{6,0},{2,4},{0,8},{4,12},{8,14},{12,10},{14,6},{10,2},{7,1},{3,5},... | collective-permute-start | bytes 368648 | tf_op jit(solution)/shard_map/ppermute | solution.py:173
  27.7 38.2 %collective-permute-start.15 = (bf16[96,640]{1,0:T(8,128)(2,1)S(1)}, bf16[96,640]{1,0:T(8,128)(2,1)}, u32[]{:S(2)}, u32[]{:S(2)}) collective-permute-start(bf16[96,640]{1,0:T(8,128)(2,1)S(1)} %copy-done.12), channel_id=1, source_target_pairs={{8,0},{12,4},{14,8},{10,12},{6,14},{2,10},{0,6},{4,2},{9,1},{13,5}... | collective-permute-start | bytes 368648 | tf_op jit(solution)/shard_map/ppermute | solution.py:173
  27.7 41.8 %collective-permute-start.18 = (bf16[96,640]{1,0:T(8,128)(2,1)S(1)}, bf16[96,640]{1,0:T(8,128)(2,1)}, u32[]{:S(2)}, u32[]{:S(2)}) collective-permute-start(bf16[96,640]{1,0:T(8,128)(2,1)S(1)} %copy-done.12), channel_id=1, source_target_pairs={{14,0},{10,4},{6,8},{2,12},{0,14},{4,10},{8,6},{12,2},{15,1},{11,5... | collective-permute-start | bytes 368648 | tf_op jit(solution)/shard_map/ppermute | solution.py:173
  37.7 33.3 %collective-permute-start.19 = (bf16[96,640]{1,0:T(8,128)(2,1)S(1)}, bf16[96,640]{1,0:T(8,128)(2,1)}, u32[]{:S(2)}, u32[]{:S(2)}) collective-permute-start(bf16[96,640]{1,0:T(8,128)(2,1)S(1)} %copy-done.12), channel_id=1, source_target_pairs={{10,0},{6,4},{2,8},{0,12},{4,14},{8,10},{12,6},{14,2},{11,1},{7,5}... | collective-permute-start | bytes 368648 | tf_op jit(solution)/shard_map/ppermute | solution.py:173
  37.7 36.9 %collective-permute-start.20 = (bf16[96,640]{1,0:T(8,128)(2,1)S(1)}, bf16[96,640]{1,0:T(8,128)(2,1)}, u32[]{:S(2)}, u32[]{:S(2)}) collective-permute-start(bf16[96,640]{1,0:T(8,128)(2,1)S(1)} %copy-done.12), channel_id=1, source_target_pairs={{12,0},{14,4},{10,8},{6,12},{2,14},{0,10},{4,6},{8,2},{13,1},{15,5... | collective-permute-start | bytes 368648 | tf_op jit(solution)/shard_map/ppermute | solution.py:173
  64.2 30.8 %collective-permute-start = (bf16[768,640]{1,0:T(8,128)(2,1)S(1)}, bf16[768,640]{1,0:T(8,128)(2,1)}, u32[]{:S(2)}, u32[]{:S(2)}) collective-permute-start(bf16[768,640]{1,0:T(8,128)(2,1)S(1)} %gather_fusion), channel_id=1, source_target_pairs={{0,4},{4,8},{8,12},{12,14},{14,10},{10,6},{6,2},{2,0},{1,5},{5,9},... | collective-permute-start | bytes 2949128 | tf_op jit(solution)/shard_map/ppermute | solution.py:173
  65.8 29.2 %collective-permute-start.2 = (bf16[768,640]{1,0:T(8,128)(2,1)S(1)}, bf16[768,640]{1,0:T(8,128)(2,1)}, u32[]{:S(2)}, u32[]{:S(2)}) collective-permute-start(bf16[768,640]{1,0:T(8,128)(2,1)S(1)} %gather_fusion), channel_id=1, source_target_pairs={{4,0},{8,4},{12,8},{14,12},{10,14},{6,10},{2,6},{0,2},{5,1},{9,5},... | collective-permute-start | bytes 2949128 | tf_op jit(solution)/shard_map/ppermute | solution.py:173
  69.4 40.7 %collective-permute-start.4 = (bf16[768,640]{1,0:T(8,128)(2,1)S(1)}, bf16[768,640]{1,0:T(8,128)(2,1)}, u32[]{:S(2)}, u32[]{:S(2)}) collective-permute-start(bf16[768,640]{1,0:T(8,128)(2,1)S(1)} %gather_fusion.1), channel_id=1, source_target_pairs={{0,4},{4,8},{8,12},{12,14},{14,10},{10,6},{6,2},{2,0},{1,5},{5,9},... | collective-permute-start | bytes 2949128 | tf_op jit(solution)/shard_map/ppermute | solution.py:173
  71.0 40.7 %collective-permute-start.6 = (bf16[768,640]{1,0:T(8,128)(2,1)S(1)}, bf16[768,640]{1,0:T(8,128)(2,1)}, u32[]{:S(2)}, u32[]{:S(2)}) collective-permute-start(bf16[768,640]{1,0:T(8,128)(2,1)S(1)} %gather_fusion.1), channel_id=1, source_target_pairs={{4,0},{8,4},{12,8},{14,12},{10,14},{6,10},{2,6},{0,2},{5,1},{9,5},... | collective-permute-start | bytes 2949128 | tf_op jit(solution)/shard_map/ppermute | solution.py:173
  74.6 8.1 %collective-permute-start.22 = (bf16[96,3456]{1,0:T(8,128)(2,1)S(1)}, bf16[96,3456]{1,0:T(8,128)(2,1)S(1)}, u32[]{:S(2)}, u32[]{:S(2)}) collective-permute-start(bf16[96,3456]{1,0:T(8,128)(2,1)S(1)} %copy-done), channel_id=1, source_target_pairs={{0,1},{1,0},{2,3},{3,2},{4,5},{5,4},{6,7},{7,6},{8,9},{9,8},{10,11... | collective-permute-start | bytes 1990664 | tf_op jit(solution)/shard_map/ppermute | solution.py:177
  82.7 2.2 collective-permute-start.21
  95.0 53.5 %collective-permute-start.1 = (bf16[768,640]{1,0:T(8,128)(2,1)}, bf16[768,640]{1,0:T(8,128)(2,1)S(1)}, u32[]{:S(2)}, u32[]{:S(2)}) collective-permute-start(bf16[768,640]{1,0:T(8,128)(2,1)} %collective-permute-done.refs_1_), channel_id=1, source_target_pairs={{0,4},{4,8},{8,12},{12,14},{14,10},{10,6},{6,2},{2,0},{1,5},{5,9},... | collective-permute-start | bytes 2949128 | tf_op jit(solution)/shard_map/ppermute | solution.py:173
  95.0 53.6 %collective-permute-start.3 = (bf16[768,640]{1,0:T(8,128)(2,1)}, bf16[768,640]{1,0:T(8,128)(2,1)S(1)}, u32[]{:S(2)}, u32[]{:S(2)}) collective-permute-start(bf16[768,640]{1,0:T(8,128)(2,1)} %collective-permute-done.2.refs_2_), channel_id=1, source_target_pairs={{4,0},{8,4},{12,8},{14,12},{10,14},{6,10},{2,6},{0,2},{5,1},{9,5},... | collective-permute-start | bytes 2949128 | tf_op jit(solution)/shard_map/ppermute | solution.py:173
  110.1 38.7 %collective-permute-start.5 = (bf16[768,640]{1,0:T(8,128)(2,1)}, bf16[768,640]{1,0:T(8,128)(2,1)}, u32[]{:S(2)}, u32[]{:S(2)}) collective-permute-start(bf16[768,640]{1,0:T(8,128)(2,1)} %collective-permute-done.4.refs_4_), channel_id=1, source_target_pairs={{0,4},{4,8},{8,12},{12,14},{14,10},{10,6},{6,2},{2,0},{1,5},{5,9},... | collective-permute-start | bytes 2949128 | tf_op jit(solution)/shard_map/ppermute | solution.py:173
  111.7 39.1 %collective-permute-start.7 = (bf16[768,640]{1,0:T(8,128)(2,1)}, bf16[768,640]{1,0:T(8,128)(2,1)S(1)}, u32[]{:S(2)}, u32[]{:S(2)}) collective-permute-start(bf16[768,640]{1,0:T(8,128)(2,1)} %collective-permute-done.6.refs_5_), channel_id=1, source_target_pairs={{4,0},{8,4},{12,8},{14,12},{10,14},{6,10},{2,6},{0,2},{5,1},{9,5},... | collective-permute-start | bytes 2949128 | tf_op jit(solution)/shard_map/ppermute | solution.py:173
  150.8 31.3 %collective-permute-start.10 = (bf16[768,640]{1,0:T(8,128)(2,1)S(1)}, bf16[768,640]{1,0:T(8,128)(2,1)S(1)}, u32[]{:S(2)}, u32[]{:S(2)}) collective-permute-start(bf16[768,640]{1,0:T(8,128)(2,1)S(1)} %collective-permute-done.1.refs_0_), channel_id=1, source_target_pairs={{0,4},{4,8},{8,12},{12,14},{14,10},{10,6},{6,2},{2,0},{1,5},{5,9},... | collective-permute-start | bytes 2949128 | tf_op jit(solution)/shard_map/ppermute | solution.py:173
  150.8 31.3 %collective-permute-start.11 = (bf16[768,640]{1,0:T(8,128)(2,1)S(1)}, bf16[768,640]{1,0:T(8,128)(2,1)S(1)}, u32[]{:S(2)}, u32[]{:S(2)}) collective-permute-start(bf16[768,640]{1,0:T(8,128)(2,1)S(1)} %collective-permute-done.3.refs_1_), channel_id=1, source_target_pairs={{4,0},{8,4},{12,8},{14,12},{10,14},{6,10},{2,6},{0,2},{5,1},{9,5},... | collective-permute-start | bytes 2949128 | tf_op jit(solution)/shard_map/ppermute | solution.py:173
  152.9 39.7 %collective-permute-start.12 = (bf16[768,640]{1,0:T(8,128)(2,1)}, bf16[768,640]{1,0:T(8,128)(2,1)S(1)}, u32[]{:S(2)}, u32[]{:S(2)}) collective-permute-start(bf16[768,640]{1,0:T(8,128)(2,1)} %collective-permute-done.5.refs_2_), channel_id=1, source_target_pairs={{0,4},{4,8},{8,12},{12,14},{14,10},{10,6},{6,2},{2,0},{1,5},{5,9},... | collective-permute-start | bytes 2949128 | tf_op jit(solution)/shard_map/ppermute | solution.py:173
  152.9 41.0 %collective-permute-start.13 = (bf16[768,640]{1,0:T(8,128)(2,1)S(1)}, bf16[768,640]{1,0:T(8,128)(2,1)S(1)}, u32[]{:S(2)}, u32[]{:S(2)}) collective-permute-start(bf16[768,640]{1,0:T(8,128)(2,1)S(1)} %collective-permute-done.7.refs_3_), channel_id=1, source_target_pairs={{4,0},{8,4},{12,8},{14,12},{10,14},{6,10},{2,6},{0,2},{5,1},{9,5},... | collective-permute-start | bytes 2949128 | tf_op jit(solution)/shard_map/ppermute | solution.py:173
  193.8 29.3 %collective-permute-start.16 = (bf16[768,640]{1,0:T(8,128)(2,1)S(1)}, bf16[768,640]{1,0:T(8,128)(2,1)S(1)}, u32[]{:S(2)}, u32[]{:S(2)}) collective-permute-start(bf16[768,640]{1,0:T(8,128)(2,1)S(1)} %collective-permute-done.10.refs_0_), channel_id=1, source_target_pairs={{0,4},{4,8},{8,12},{12,14},{14,10},{10,6},{6,2},{2,0},{1,5},{5,9},... | collective-permute-start | bytes 2949128 | tf_op jit(solution)/shard_map/ppermute | solution.py:173
  193.8 29.3 %collective-permute-start.17 = (bf16[768,640]{1,0:T(8,128)(2,1)S(1)}, bf16[768,640]{1,0:T(8,128)(2,1)S(1)}, u32[]{:S(2)}, u32[]{:S(2)}) collective-permute-start(bf16[768,640]{1,0:T(8,128)(2,1)S(1)} %collective-permute-done.13.refs_3_), channel_id=1, source_target_pairs={{4,0},{8,4},{12,8},{14,12},{10,14},{6,10},{2,6},{0,2},{5,1},{9,5},... | collective-permute-start | bytes 2949128 | tf_op jit(solution)/shard_map/ppermute | solution.py:173
  (15 other events, 199.5 us)
Sparse Core Ops, SparseCore 0:
  9.6 58.1 all-gather.1
